TPU v7x, 32 devices: a whole 2x2x4 slice. The times are simulated.
32 devices in a mesh: grp: 8 (over z, x), tp: 4 (over y, core).
Axes of the slice: x: 2, y: 2, z: 4, core: 2. Of those that a mesh axis runs over, the one named last changes fastest.
Arguments:
- features: bfloat16 [96, 128, 8192], P('grp', None, 'tp'), may hold values from -6 to 6
- tile_request: int32 [96], P('grp'), may hold values from 0 to 63, as said below
- tile_rows: int32 [96], P('grp'), may hold values from 0 to 128, as said below
- key_weight: bfloat16 [8192, 1024], P('tp'), may hold values from -0.0625 to 0.0625
- value_weight: bfloat16 [8192, 1024], P('tp'), may hold values from -0.0625 to 0.0625
- key_gain: float32 [128], replicated, may hold values from 0.1 to 1.9
- cached_keys: bfloat16 [64, 512, 1024], P('grp', None, 'tp'), may hold values from -3 to 3
- cached_values: bfloat16 [64, 512, 1024], P('grp', None, 'tp'), may hold values from -6 to 6
- cache_len: int32 [64], P('grp'), may hold values from 2 to 512, as said below
- queries: bfloat16 [2, 64, 8192], P(None, 'grp', 'tp'), may hold values from -8 to 8
Outputs:
- context: bfloat16 [2, 64, 8192], P(None, 'grp', 'tp')
Inputs may be any that keep to these rules, and one draw needn't show every extreme that they name: `tile_request`: request r belongs to decode group r // 8. The 12 tiles of one encoder device (aligned blocks) hold at most 2 tiles for one decode group, and at most 16 tiles in all serve one group's requests; both bounds are reached in every draw. A group's tiles are spread evenly over its requests, so no request has more than 2 tiles, rounded up. `tile_rows`: A tile is either live in all 128 rows or a padding tile with 0 live rows. `cache_len`: cached positions at or past a request's count are unused.
All inputs are finite; a program needn't handle non-finite values.
Results may differ from a plain program's by a relative error of at most 0.0059.
Values may be sent and summed in bfloat16 or wider, within the bound.
A program may use at most 128 MiB of HBM per device.

v0:
```python
import jax
import jax.numpy as jnp
from jax import lax
from jax.sharding import PartitionSpec as P

KVH = 8
NH = 64
HD = 128


EPSILON = 1e-05


def key_norm(raw_rows, gain):
    scale = lax.rsqrt(jnp.mean(raw_rows * raw_rows, axis=-1, keepdims=True) + EPSILON)
    return raw_rows * scale * gain


def attend(
    query_block, cache_keys, cache_values, cache_count, new_keys, new_values, new_request, new_count
):
    factor = query_block.shape[-1] ** (-0.5)
    cache_scores = (
        jnp.einsum("srhgd,rchd->srhgc", query_block, cache_keys, preferred_element_type=jnp.float32)
        * factor
    )
    new_scores = (
        jnp.einsum("srhgd,nthd->srhgnt", query_block, new_keys, preferred_element_type=jnp.float32)
        * factor
    )
    requests_here = query_block.shape[1]
    cache_mask = jnp.arange(cache_keys.shape[1])[None, :] < cache_count[:, None]
    cache_mask = cache_mask[None, :, None, None, :]
    row_live = jnp.arange(new_keys.shape[1])[None, :] < new_count[:, None]
    belongs = new_request[None, :] == jnp.arange(requests_here)[:, None]
    new_mask = (belongs[:, :, None] & row_live[None, :, :])[None, :, None, None, :, :]
    floor_value = -1e30
    cache_masked = jnp.where(cache_mask, cache_scores, floor_value)
    new_masked = jnp.where(new_mask, new_scores, floor_value)
    row_peak = jnp.maximum(jnp.max(cache_masked, axis=-1), jnp.max(new_masked, axis=(-2, -1)))
    cache_exp = jnp.where(cache_mask, jnp.exp(cache_masked - row_peak[..., None]), 0.0)
    new_exp = jnp.where(new_mask, jnp.exp(new_masked - row_peak[..., None, None]), 0.0)
    denominator = jnp.sum(cache_exp, axis=-1) + jnp.sum(new_exp, axis=(-2, -1))
    cache_weights = (cache_exp / denominator[..., None]).astype(jnp.bfloat16)
    new_weights = (new_exp / denominator[..., None, None]).astype(jnp.bfloat16)
    context = jnp.einsum(
        "srhgc,rchd->srhgd", cache_weights, cache_values, preferred_element_type=jnp.float32
    )
    context = context + jnp.einsum(
        "srhgnt,nthd->srhgd", new_weights, new_values, preferred_element_type=jnp.float32
    )
    return context.astype(jnp.bfloat16)


def project(flat_rows, key_weight, value_weight):
    row_total = flat_rows.shape[0]
    part_keys = jnp.dot(flat_rows, key_weight, preferred_element_type=jnp.float32).reshape(
        row_total, KVH, HD
    )
    part_values = jnp.dot(flat_rows, value_weight, preferred_element_type=jnp.float32).reshape(
        row_total, KVH, HD
    )
    return (part_keys, part_values)


def on_device(
    features,
    tile_request,
    tile_rows,
    key_weight,
    value_weight,
    key_gain,
    cached_keys,
    cached_values,
    cache_len,
    queries,
):
    groups = lax.axis_size("grp")
    tensor = lax.axis_size("tp")
    tiles_dev, tile_len, feat_cols = features.shape
    heads_local = KVH // tensor
    group_size = NH // KVH
    steps_here = queries.shape[0]
    requests_dev = cache_len.shape[0]
    cache_slots = cached_keys.shape[1]
    peer_slots = -(-tiles_dev // groups)
    capacity = min(2 * tiles_dev, groups * peer_slots)
    slot_total = groups * peer_slots
    my_group = lax.axis_index("grp")
    all_requests, all_rows = (
        lax.all_gather(tile_request, "grp", axis=0, tiled=True),
        lax.all_gather(tile_rows, "grp", axis=0, tiled=True),
    )
    all_requests = all_requests.reshape(groups, tiles_dev)
    all_rows = all_rows.reshape(groups, tiles_dev)
    earlier = jnp.arange(tiles_dev)[None, :] < jnp.arange(tiles_dev)[:, None]
    own_target = tile_request // requests_dev
    own_rank = jnp.sum((own_target[:, None] == own_target[None, :]) & earlier, axis=1)
    slot_ids = own_target * peer_slots + own_rank
    send_select = slot_ids[None, :] == jnp.arange(slot_total)[:, None]
    send_present = jnp.any(send_select, axis=1)
    send_source = jnp.sum(jnp.where(send_select, jnp.arange(tiles_dev)[None, :], 0), axis=1)
    all_target = all_requests // requests_dev
    all_rank = jnp.sum((all_target[:, :, None] == all_target[:, None, :]) & earlier[None], axis=2)
    matches = (all_target[:, None, :] == my_group) & (
        all_rank[:, None, :] == jnp.arange(peer_slots)[None, :, None]
    )
    recv_present = jnp.any(matches, axis=2).reshape(slot_total)
    recv_request = (
        jnp.sum(jnp.where(matches, all_requests[:, None, :], 0), axis=2).reshape(slot_total)
        - my_group * requests_dev
    )
    recv_rows = jnp.sum(jnp.where(matches, all_rows[:, None, :], 0), axis=2).reshape(slot_total)
    position = jnp.cumsum(recv_present.astype(jnp.int32)) - 1
    pick_table = recv_present[None, :] & (position[None, :] == jnp.arange(capacity)[:, None])
    kept_slot = jnp.any(pick_table, axis=1)
    pick_source = jnp.sum(jnp.where(pick_table, jnp.arange(slot_total)[None, :], 0), axis=1)
    new_request = jnp.where(kept_slot, recv_request[pick_source], -1)
    new_count = jnp.where(kept_slot, recv_rows[pick_source], 0)
    outgoing = jnp.where(send_present[:, None, None], features[send_source], 0)
    outgoing = outgoing.reshape(groups, peer_slots, tile_len, feat_cols)
    arrived = lax.all_to_all(outgoing, "grp", split_axis=0, concat_axis=0, tiled=True)
    arrived = arrived.reshape(slot_total, tile_len, feat_cols)[pick_source]
    part_keys, part_values = project(
        arrived.reshape(capacity * tile_len, feat_cols), key_weight, value_weight
    )
    sum_keys, sum_values = (
        lax.psum_scatter(part_keys, "tp", scatter_dimension=1, tiled=True),
        lax.psum_scatter(part_values, "tp", scatter_dimension=1, tiled=True),
    )
    new_keys = (
        key_norm(sum_keys, key_gain)
        .astype(jnp.bfloat16)
        .reshape(capacity, tile_len, heads_local, HD)
    )
    new_values = sum_values.astype(jnp.bfloat16).reshape(capacity, tile_len, heads_local, HD)
    query_block = queries.reshape(steps_here, requests_dev, heads_local, group_size, HD)
    cache_block = cached_keys.reshape(requests_dev, cache_slots, heads_local, HD)
    value_block = cached_values.reshape(requests_dev, cache_slots, heads_local, HD)
    context = attend(
        query_block,
        cache_block,
        value_block,
        cache_len,
        new_keys,
        new_values,
        new_request,
        new_count,
    )
    return context.reshape(steps_here, requests_dev, heads_local * group_size * HD)


def solution(mesh):
    in_specs = (
        P("grp", None, "tp"),
        P("grp"),
        P("grp"),
        P("tp", None),
        P("tp", None),
        P(),
        P("grp", None, "tp"),
        P("grp", None, "tp"),
        P("grp"),
        P(None, "grp", "tp"),
    )
    out_specs = P(None, "grp", "tp")
    return jax.shard_map(
        on_device, mesh=mesh, in_specs=in_specs, out_specs=out_specs, check_vma=False
    )
```

profile of v0, /device:TPU:0, one launch (start us, length us, event | category | flops | bytes accessed | tf_op | source)
XLA Modules:
  0.0 400.7 jit_solution(16506606966814567498)
XLA Ops:
  6.5 0.7 and_select_fusion
  7.2 0.2 convert_reduce_fusion.1
  7.4 0.7 multiply_add_fusion
  8.1 0.1 select_reduce_fusion
  8.2 0.1 fusion.33
  8.3 0.1 broadcast_in_dim.146
  8.4 7.5 %gather_fusion.2 = bf16[16,128,2048]{2,1,0:T(8,128)(2,1)} fusion(bf16[12,128,2048]{2,1,0:T(8,128)(2,1)} %param.10, s32[1024]{0:T(1024)S(1)} %pad_clamp_fusion), kind=kCustom, calls=%fused_computation.2 | custom fusion | bytes 16777280 | tf_op jit(solution)/shard_map/gather | solution.py:120
  15.9 7.2 %broadcast_select_fusion = bf16[8,2,128,2048]{3,2,1,0:T(8,128)(2,1)} fusion(bf16[8,2,128,2048]{3,2,1,0:T(8,128)(2,1)} %bitcast.68, pred[8,2]{1,0:T(8,128)(4,1)S(1)} %broadcast_in_dim.146), kind=kLoop, calls=%fused_computation.4 | loop fusion | flops 4194304 | bytes 16777232 | tf_op jit(solution)/shard_map/jit(_where)/select_n | solution.py:120
  23.2 7.4 %all-to-all-start = ((bf16[8,2,128,2048]{3,2,1,0:T(8,128)(2,1)}), bf16[8,2,128,2048]{3,2,1,0:T(8,128)(2,1)}, u32[]{:S(2)}, u32[]{:S(2)}) async-start(bf16[8,2,128,2048]{3,2,1,0:T(8,128)(2,1)} %broadcast_select_fusion), calls=%async_computation | async-start | bytes 16777216 | tf_op jit(solution)/shard_map/all_to_all | solution.py:122
  30.6 0.6 dynamic-slice
  31.9 0.2 dynamic-update-slice
  32.1 0.2 dynamic-update-slice.1
  32.3 181.5 %all-reduce.2 = (s32[96]{0:T(128)S(1)}, s32[96]{0:T(128)S(1)}) all-reduce(s32[96]{0:T(128)S(1)} %dynamic-update-slice, s32[96]{0:T(128)S(1)} %dynamic-update-slice.1), channel_id=1, replica_groups=mesh['grp'=8,'tp'=4] {'grp'}, use_global_device_ids=true, to_apply=%add | all-reduce | flops 192 | bytes 1536
  213.9 0.1 copy.79
  214.0 0.3 convert_reduce_fusion
  214.5 0.2 fusion.35
  214.6 0.1 copy.81
  214.9 0.1 and.84
  215.0 6.5 %copy.108 = bf16[1024,2048]{1,0:T(8,128)(2,1)} copy(bf16[1024,2048]{0,1:T(8,128)(2,1)} %bitcast.72) | data formatting | bytes 8388608 | tf_op jit(solution)/shard_map/dot_general | solution.py:57
  221.5 0.1 add_reduce_fusion
  221.6 0.1 select_reduce_fusion.2
  221.7 8.1 %gather_fusion.3 = bf16[16,128,2048]{2,1,0:T(8,128)(2,1)} fusion(bf16[16,128,2048]{2,1,0:T(8,128)(2,1)} %bitcast.9, s32[1024]{0:T(1024)S(1)} %pad_clamp_fusion.1), kind=kCustom, calls=%fused_computation.3 | custom fusion | bytes 16777280 | tf_op jit(solution)/shard_map/gather | solution.py:123
  229.8 13.9 %fusion.44 = f32[2048,8,128]{2,0,1:T(8,128)} fusion(bf16[2048,2048,1]{1,0,2:T(8,128)(2,1)} %bitcast.69, bf16[8,128,2048]{2,1,0:T(8,128)(2,1)} %bitcast.74), kind=kOutput, calls=%fused_computation.81 | convolution fusion | flops 8589934592 | bytes 20971520 | tf_op jit(solution)/shard_map/dot_general | solution.py:57
  243.8 0.2 reduce-scatter.5.cloned.1.call-start
  244.0 6.6 %copy.113 = bf16[1024,2048]{1,0:T(8,128)(2,1)} copy(bf16[1024,2048]{0,1:T(8,128)(2,1)} %bitcast.73) | data formatting | bytes 8388608 | tf_op jit(solution)/shard_map/dot_general | solution.py:60
  250.7 15.7 %fusion.45 = f32[2048,8,128]{2,0,1:T(8,128)} fusion(bf16[2048,2048,1]{1,0,2:T(8,128)(2,1)} %bitcast.70, bf16[8,128,2048]{2,1,0:T(8,128)(2,1)} %bitcast.75), kind=kOutput, calls=%fused_computation.82 | convolution fusion | flops 8589934592 | bytes 20971520 | tf_op jit(solution)/shard_map/dot_general | solution.py:60
  266.4 0.1 select_reduce_fusion.3
  266.6 0.1 copy.84
  266.7 0.1 sub.45
  266.8 0.7 gather_fusion
  267.6 0.7 gather_fusion.1
  268.3 2.1 reshape.286
  270.3 4.1 %reshape.293 = bf16[8,512,2,128]{3,2,1,0:T(2,128)(2,1)} reshape(bf16[8,512,256]{2,1,0:T(8,128)(2,1)} %param.17) | data formatting | bytes 4194304 | tf_op jit(solution)/shard_map/reshape | solution.py:139
  274.5 0.1 fusion.37
  274.8 0.1 broadcast_and_fusion
  274.9 0.8 fusion.43
  275.7 39.1 %reduce-scatter.3.cloned.1.call-done = f32[2048,2,128]{2,0,1:T(8,128)} async-done(((f32[2048,8,128]{2,0,1:T(8,128)}), f32[2048,2,128]{2,0,1:T(8,128)}) %reduce-scatter.3.cloned.1.call-update) | async-done | bytes 2097168 | tf_op jit(solution)/shard_map/reduce_scatter | solution.py:128
  314.8 2.4 multiply_reduce_fusion
  317.2 0.7 multiply_convert_fusion
  318.0 0.6 fusion.4
  318.6 0.3 fusion.25
  318.9 0.8 fusion.5
  319.7 69.6 %reduce-scatter.5.cloned.1.call-done = f32[2048,2,128]{2,0,1:T(8,128)} async-done(((f32[2048,8,128]{2,0,1:T(8,128)}), f32[2048,2,128]{2,0,1:T(8,128)}) %reduce-scatter.5.cloned.1.call-update) | async-done | bytes 2097168 | tf_op jit(solution)/shard_map/reduce_scatter | solution.py:129
  389.3 1.7 convert_element_type.44
  391.0 0.8 convolution_bitcast_fusion
  391.9 0.7 copy-done.3
  392.6 0.5 fusion.21
  393.2 0.7 reshape.295
  (51 shorter events, 1.1 us)
Async XLA Ops:
  6.5 268.4 %copy-start = (bf16[2,8,2048]{2,1,0:T(8,128)(2,1)S(1)}, bf16[2,8,2048]{2,1,0:T(8,128)(2,1)}, u32[]{:S(2)}) copy-start(bf16[2,8,2048]{2,1,0:T(8,128)(2,1)} %param.19) | copy-start | bytes 196612
  23.1 7.4 %copy-start.9 = (u32[32]{0:T(128)S(1)}, u32[32]{0:T(128)}, u32[]{:S(2)}) copy-start(u32[32]{0:T(128)} %constant.69) | copy-start | bytes 388
  23.1 8.7 %copy-start.7 = (s32[12]{0:T(128)S(1)}, s32[12]{0:T(128)}, u32[]{:S(2)}) copy-start(s32[12]{0:T(128)} %param.11) | copy-start | bytes 148
  23.1 8.9 %copy-start.8 = (s32[12]{0:T(128)S(1)}, s32[12]{0:T(128)}, u32[]{:S(2)}) copy-start(s32[12]{0:T(128)} %param.12) | copy-start | bytes 148
  23.2 198.6 %all-to-all-start = ((bf16[8,2,128,2048]{3,2,1,0:T(8,128)(2,1)}), bf16[8,2,128,2048]{3,2,1,0:T(8,128)(2,1)}, u32[]{:S(2)}, u32[]{:S(2)}) async-start(bf16[8,2,128,2048]{3,2,1,0:T(8,128)(2,1)} %broadcast_select_fusion), calls=%async_computation | async-start | bytes 16777216 | tf_op jit(solution)/shard_map/all_to_all | solution.py:122
  30.5 284.3 %reduce-scatter.3.cloned.1.call-start = ((), (), s32[]{:S(2)}) async-start(), calls=%async_computation.3 | async-start | bytes 10485760 | tf_op jit(solution)/shard_map/reduce_scatter | solution.py:128
  243.8 145.5 %reduce-scatter.5.cloned.1.call-start = ((), (), s32[]{:S(2)}) async-start(), calls=%async_computation.4 | async-start | bytes 10485760 | tf_op jit(solution)/shard_map/reduce_scatter | solution.py:129
  266.3 1.9 copy-start.2
  270.3 4.4 %copy-start.5 = (s32[8]{0:T(128)S(1)}, s32[8]{0:T(128)}, u32[]{:S(2)}) copy-start(s32[8]{0:T(128)} %param.18) | copy-start | bytes 100
  270.3 4.6 %copy-start.4 = (bf16[8,512,2,128]{3,2,1,0:T(2,128)(2,1)S(1)}, bf16[8,512,2,128]{3,2,1,0:T(2,128)(2,1)}, u32[]{:S(2)}) copy-start(bf16[8,512,2,128]{3,2,1,0:T(2,128)(2,1)} %reshape.286) | copy-start | bytes 6291460
  274.9 42.3 %copy-start.6 = (f32[128]{0:T(128)S(1)}, f32[128]{0:T(128)}, u32[]{:S(2)}) copy-start(f32[128]{0:T(128)} %param.15) | copy-start | bytes 1540
  314.8 2.4 copy-start.1
  391.0 1.6 copy-start.3
Sparse Core Ops, SparseCore 0:
  243.9 70.8 reduce-scatter.2
  317.6 71.6 reduce-scatter.4
where the time goes:
time: 401 us
  blocking collectives  182 us (45%)
  waiting for transfers between devices  109 us (27%)
  local copies, waits for them, and re-layouts  39.9 us (10%)
  matrix products  32.3 us (8%)
  other arithmetic  16.3 us (4%)
  between operations  14.3 us (4%)
  starting transfers between devices  7.64 us (2%)
    unnamed x1, blocking collectives  182 us
    reduce_scatter x1, waiting for transfers between devices, on_device(): lax.psum_scatter(part_values, 'tp', scatter_dimension=1, tiled=True)  69.6 us
    reduce_scatter x1, waiting for transfers between devices, on_device(): lax.psum_scatter(part_keys, 'tp', scatter_dimension=1, tiled=True)  39.1 us
    dot_general x1, matrix products, project(): jnp.dot(flat_rows, value_weight, preferred_element_type=jnp.float32)  15.7 us
    dot_general x1, matrix products, project(): jnp.dot(flat_rows, key_weight, preferred_element_type=jnp.float32)  13.9 us
    gather x1, local copies, waits for them, and re-layouts, on_device(): arrived = arrived.reshape(slot_total, tile_len, feat_cols)[pick_source]  8.11 us
  transfers between devices with their start and end apart: 3, of which 2 were waited for; matrix products, arithmetic and copies ran while one was open for 11% of the time, Pallas kernels for 0%

commit v1 on v0

v1 whole, which is shorter than its diff:
```python
import jax
import jax.numpy as jnp
from jax import lax
from jax.sharding import PartitionSpec as P

KVH = 8
NH = 64
HD = 128
EPSILON = 1e-05
FLOOR = -1e30


def key_norm(raw_rows, gain):
    scale = lax.rsqrt(jnp.mean(raw_rows * raw_rows, axis=-1, keepdims=True) + EPSILON)
    return raw_rows * scale * gain


def split_attend(scores, mask, values, spec):
    masked = jnp.where(mask, scores, FLOOR)
    peak = jnp.max(masked, axis=-1, keepdims=True)
    weights = jnp.where(mask, jnp.exp(masked - peak), 0.0)
    total = jnp.sum(weights, axis=-1, keepdims=True)
    out = jnp.einsum(spec, weights.astype(jnp.bfloat16), values, preferred_element_type=jnp.float32)
    live = total > 0
    safe = jnp.where(live, total, 1.0)
    return out / safe, jnp.where(live, peak + jnp.log(safe), FLOOR)


def on_device(
    features, tile_request, tile_rows, key_weight, value_weight, key_gain,
    cached_keys, cached_values, cache_len, queries,
):
    groups = lax.axis_size("grp")
    tensor = lax.axis_size("tp")
    tiles, tile_len, feat_cols = features.shape
    heads = KVH // tensor
    per = NH // KVH
    steps = queries.shape[0]
    requests = cache_len.shape[0]
    cache_slots = cached_keys.shape[1]
    peer_slots = -(-tiles // groups)
    slot_total = groups * peer_slots
    me = lax.axis_index("grp")
    factor = HD ** (-0.5)

    all_q = lax.all_gather(queries, "grp", axis=0, tiled=False)
    all_req = lax.all_gather(tile_request, "grp", axis=0, tiled=False)
    flat = features.reshape(tiles * tile_len, feat_cols)
    part_keys = jnp.dot(flat, key_weight, preferred_element_type=jnp.float32)
    part_values = jnp.dot(flat, value_weight, preferred_element_type=jnp.float32)
    sum_keys = lax.psum_scatter(part_keys, "tp", scatter_dimension=1, tiled=True)
    sum_values = lax.psum_scatter(part_values, "tp", scatter_dimension=1, tiled=True)
    new_keys = key_norm(sum_keys.reshape(tiles, tile_len, heads, HD), key_gain).astype(jnp.bfloat16)
    new_values = sum_values.astype(jnp.bfloat16).reshape(tiles, tile_len, heads, HD)

    q_all = all_q.transpose(0, 2, 1, 3).reshape(groups * requests, steps, heads, per, HD)
    q_tile = q_all[tile_request]
    scores = jnp.einsum("nshgd,nthd->nhsgt", q_tile, new_keys, preferred_element_type=jnp.float32) * factor
    mask = (jnp.arange(tile_len)[None, :] < tile_rows[:, None])[:, None, None, None, :]
    tile_out, tile_lse = split_attend(scores, mask, new_values, "nhsgt,nthd->nhsgd")

    earlier = jnp.arange(tiles)[None, :] < jnp.arange(tiles)[:, None]
    target = tile_request // requests
    rank = jnp.sum((target[:, None] == target[None, :]) & earlier, axis=1)
    slot = target * peer_slots + rank
    select = slot[None, :] == jnp.arange(slot_total)[:, None]
    present = jnp.any(select, axis=1)
    source = jnp.sum(jnp.where(select, jnp.arange(tiles)[None, :], 0), axis=1)
    out_slots = tile_out[source]
    lse_slots = jnp.where(present[:, None, None, None, None], tile_lse[source], FLOOR)
    payload = jnp.concatenate([out_slots, lse_slots], axis=-1)
    got = lax.all_to_all(payload, "grp", split_axis=0, concat_axis=0, tiled=True)
    got_out, got_lse = got[..., :HD], got[..., HD:]

    all_target = all_req // requests
    all_rank = jnp.sum((all_target[:, :, None] == all_target[:, None, :]) & earlier[None], axis=2)
    hit = (all_target[:, None, :] == me) & (all_rank[:, None, :] == jnp.arange(peer_slots)[None, :, None])
    slot_req = jnp.where(jnp.any(hit, axis=2), jnp.sum(jnp.where(hit, all_req[:, None, :] - me * requests, 0), axis=2), -1)
    slot_req = slot_req.reshape(slot_total)

    q_block = queries.reshape(steps, requests, heads, per, HD)
    c_keys = cached_keys.reshape(requests, cache_slots, heads, HD)
    c_values = cached_values.reshape(requests, cache_slots, heads, HD)
    c_scores = jnp.einsum("srhgd,rchd->rhsgc", q_block, c_keys, preferred_element_type=jnp.float32) * factor
    c_mask = (jnp.arange(cache_slots)[None, :] < cache_len[:, None])[:, None, None, None, :]
    c_out, c_lse = split_attend(c_scores, c_mask, c_values, "rhsgc,rchd->rhsgd")

    belongs = (slot_req[None, :] == jnp.arange(requests)[:, None])[:, :, None, None, None, None]
    r_lse = jnp.where(belongs, got_lse[None], FLOOR)
    peak = jnp.maximum(c_lse, jnp.max(r_lse, axis=1))
    c_w = jnp.exp(c_lse - peak)
    r_w = jnp.where(belongs, jnp.exp(r_lse - peak[:, None]), 0.0)
    num = c_w * c_out + jnp.sum(jnp.where(belongs, r_w * got_out[None], 0.0), axis=1)
    den = c_w + jnp.sum(r_w, axis=1)
    context = (num / den).astype(jnp.bfloat16)
    return context.transpose(2, 0, 1, 3, 4).reshape(steps, requests, heads * per * HD)


def solution(mesh):
    in_specs = (
        P("grp", None, "tp"), P("grp"), P("grp"), P("tp", None), P("tp", None), P(),
        P("grp", None, "tp"), P("grp", None, "tp"), P("grp"), P(None, "grp", "tp"),
    )
    return jax.shard_map(
        on_device, mesh=mesh, in_specs=in_specs, out_specs=P(None, "grp", "tp"), check_vma=False
    )
```

time: 401 us -> 176 us (0.44)
  blocking collectives: 182 us -> 43.9 us
  waiting for transfers between devices: 109 us -> 63.5 us
  local copies, waits for them, and re-layouts: 39.9 us -> 12.5 us
  other arithmetic: 16.3 us -> 9.6 us
  matrix products: 32.3 us -> 25.8 us
    unnamed x1, blocking collectives: 182 us -> 10.8 us
    reduce_scatter x1, waiting for transfers between devices: 39.1 us -> 0.01 us  [on_device(): lax.psum_scatter(part_keys, 'tp', scatter_dimension=1, tiled=True)]
    all_gather x0 -> x1, blocking collectives: none -> 33.1 us  [on_device(): all_q = lax.all_gather(queries, 'grp', axis=0, tiled=False)]
    reduce_scatter x1, waiting for transfers between devices: 69.6 us -> 51.5 us  [on_device(): lax.psum_scatter(part_values, 'tp', scatter_dimension=1, tiled=True)]
    gather x4, local copies, waits for them, and re-layouts: 17 us -> 2.17 us  [the longest x2 1.04 us: on_device(): tile_lse[source]]
    dot_general x2 -> x0, local copies, waits for them, and re-layouts: 13.1 us -> none  [the longest x1 6.64 us: project(): jnp.dot(flat_rows, value_weight, preferred_element_type=jnp.float32)]
    all_to_all x1, waiting for transfers between devices: 0.01 us -> 12 us  [on_device(): lax.all_to_all(payload, 'grp', split_axis=0, concat_axis=0, tiled=True)]
    select_n x5 -> x7, other arithmetic: 7.91 us -> 0.44 us  [the longest x1 0.28 us: on_device(): r_w = jnp.where(belongs, jnp.exp(r_lse - peak[:, None]), 0.0)]
  transfers between devices with their start and end apart: 3 -> 3, of which waited for: 2 -> 2; matrix products, arithmetic and copies ran while one was open for 11% -> 16% of each run, Pallas kernels for 0% -> 0%
where the time goes in v1:
time: 176 us; the launch traced here: 175 us
  waiting for transfers between devices  63.5 us (36%)
  blocking collectives  43.9 us (25%)
  matrix products  25.8 us (15%)
  between operations  14.4 us (8%)
  local copies, waits for them, and re-layouts  12.5 us (7%)
  other arithmetic  9.6 us (5%)
  starting transfers between devices  5.53 us (3%)
    reduce_scatter x1, waiting for transfers between devices, on_device(): lax.psum_scatter(part_values, 'tp', scatter_dimension=1, tiled=True)  51.5 us
    all_gather x1, blocking collectives, on_device(): all_q = lax.all_gather(queries, 'grp', axis=0, tiled=False)  33.1 us
    all_to_all x1, waiting for transfers between devices, on_device(): lax.all_to_all(payload, 'grp', split_axis=0, concat_axis=0, tiled=True)  12 us
    dot_general x1, matrix products, on_device(): jnp.dot(flat, value_weight, preferred_element_type=jnp.float32)  11.9 us
    dot_general x1, matrix products, on_device(): part_keys = jnp.dot(flat, key_weight, preferred_element_type=jnp.float32)  11.7 us
    unnamed x1, blocking collectives  10.8 us
    all_to_all x1, starting transfers between devices, on_device(): lax.all_to_all(payload, 'grp', split_axis=0, concat_axis=0, tiled=True)  5.49 us
  transfers between devices with their start and end apart: 3, of which 2 were waited for; matrix products, arithmetic and copies ran while one was open for 16% of the time, Pallas kernels for 0%

profile of v1, /device:TPU:0, one launch (start us, length us, event | category | flops | bytes accessed | tf_op | source)
XLA Modules:
  0.0 175.2 jit_solution(1296915865512227594)
XLA Ops:
  6.5 11.7 %fusion.67 = f32[1536,1024]{1,0:T(8,128)} fusion(bf16[1536,2048]{1,0:T(8,128)(2,1)} %bitcast.80, bf16[2048,1024]{1,0:T(8,128)(2,1)} %param.13), kind=kOutput, calls=%fused_computation.101 | convolution fusion | flops 6442450944 | bytes 16777216 | tf_op jit(solution)/shard_map/dot_general | solution.py:49
  18.3 11.9 %fusion.68 = f32[1536,1024]{1,0:T(8,128)} fusion(bf16[1536,2048]{1,0:T(8,128)(2,1)} %bitcast.81, bf16[2048,1024]{1,0:T(8,128)(2,1)} %param.14), kind=kOutput, calls=%fused_computation.102 | convolution fusion | flops 6442450944 | bytes 16777216 | tf_op jit(solution)/shard_map/dot_general | solution.py:50
  30.3 0.8 copy-done.2
  31.1 33.1 %all-gather.1 = bf16[16,8,2048]{2,1,0:T(8,128)(2,1)S(1)} all-gather(bf16[2,8,2048]{2,1,0:T(8,128)(2,1)S(1)} %copy-done.2), channel_id=3, replica_groups=mesh['grp'=8,'tp'=4] {'grp'}, dimensions={0}, use_global_device_ids=true | all-gather | bytes 589824 | tf_op jit(solution)/shard_map/all_gather | solution.py:46
  64.2 0.1 copy.105
  64.4 0.6 dynamic-slice
  65.7 0.2 dynamic-update-slice
  65.9 10.8 %all-reduce = s32[96]{0:T(128)S(1)} all-reduce(s32[96]{0:T(128)S(1)} %dynamic-update-slice), channel_id=2, replica_groups=mesh['grp'=8,'tp'=4] {'grp'}, use_global_device_ids=true, to_apply=%add | all-reduce | flops 96 | bytes 768
  76.7 0.1 reshape.277
  76.8 0.1 copy.75
  76.9 0.3 convert_reduce_fusion
  77.3 2.6 %reshape.244 = bf16[8,512,2,128]{3,2,1,0:T(2,128)(2,1)S(1)} reshape(bf16[8,512,256]{2,1,0:T(8,128)(2,1)} %param.16) | data formatting | bytes 4194304 | tf_op jit(solution)/shard_map/reshape | solution.py:82
  80.0 0.6 gather_fusion
  80.5 0.2 convert_reduce_fusion.1
  80.7 0.1 select_reduce_fusion.2
  80.9 0.1 fusion.56
  81.0 0.1 fusion.58
  81.1 0.1 select_reduce_fusion.3
  81.5 0.8 fusion.65
  82.2 2.1 %reshape.247 = f32[12,128,2,128]{3,2,1,0:T(2,128)S(1)} reshape(f32[1536,256]{1,0:T(8,128)} %reduce-scatter.3.cloned.1.call-done) | data formatting | bytes 3145728 | tf_op jit(solution)/shard_map/reshape | solution.py:53
  84.3 1.7 multiply_reduce_fusion
  86.0 0.1 add_rsqrt_fusion
  86.1 1.9 %fusion.29 = bf16[12,128,2,128,1]{3,2,1,0,4:T(2,128)(2,1)S(1)} fusion(f32[12,128,2,128]{3,2,1,0:T(2,128)S(1)} %reshape.247, f32[128]{0:T(128)S(1)} %copy-done.5, f32[12,128,2]{2,1,0:T(8,128)S(1)} %add_rsqrt_fusion), kind=kLoop, calls=%fused_computation.21 | loop fusion | flops 1179648 | bytes 2372096 | tf_op jit(solution)/shard_map/convert_element_type | solution.py:53
  88.1 0.6 fusion.66
  88.7 0.3 fusion.38
  89.0 51.5 %reduce-scatter.5.cloned.1.call-done = f32[1536,256]{1,0:T(8,128)} async-done(((f32[1536,1024]{1,0:T(8,128)}), f32[1536,256]{1,0:T(8,128)}) %reduce-scatter.5.cloned.1.call-update) | async-done | bytes 1572880 | tf_op jit(solution)/shard_map/reduce_scatter | solution.py:52
  140.5 1.5 convert_element_type.25
  142.0 0.2 reshape.248
  142.2 0.4 convolution_divide_fusion
  142.6 0.6 gather_fusion.1
  143.2 0.6 gather_fusion.2
  143.8 0.4 copy.86
  144.2 0.1 broadcast_select_fusion
  144.3 0.8 pad_maximum_fusion
  145.2 5.5 %all-to-all-start = ((f32[16,2,2,8,129]{4,3,2,1,0:T(8,128)}), f32[16,2,2,8,129]{4,3,2,1,0:T(8,128)S(1)}, u32[]{:S(2)}, u32[]{:S(2)}) async-start(f32[16,2,2,8,129]{4,3,2,1,0:T(8,128)} %pad_maximum_fusion), calls=%async_computation.2 | async-start | bytes 1048576 | tf_op jit(solution)/shard_map/all_to_all | solution.py:72
  150.7 0.1 copy.77
  150.7 0.1 select_n.187
  150.8 2.1 %reshape.249 = bf16[8,512,2,128]{3,2,1,0:T(2,128)(2,1)} reshape(bf16[8,512,256]{2,1,0:T(8,128)(2,1)S(1)} %copy-done) | data formatting | bytes 4194304 | tf_op jit(solution)/shard_map/reshape | solution.py:83
  152.9 0.3 fusion.33
  153.2 12.0 %all-to-all-done = f32[16,2,2,8,129]{4,3,2,1,0:T(8,128)S(1)} async-done(((f32[16,2,2,8,129]{4,3,2,1,0:T(8,128)}), f32[16,2,2,8,129]{4,3,2,1,0:T(8,128)S(1)}, u32[]{:S(2)}, u32[]{:S(2)}) %all-to-all-start) | async-done | bytes 264224 | tf_op jit(solution)/shard_map/all_to_all | solution.py:72
  165.2 0.3 copy.87
  165.4 0.1 copy.89
  165.5 0.1 select_reduce_fusion.1
  165.7 0.2 fusion.42
  166.0 0.3 exponential_select_fusion.1
  166.3 0.9 select_reduce_fusion
  167.2 0.5 fusion.26
  167.7 0.7 reshape.250
  (43 shorter events, 0.7 us)
Async XLA Ops:
  6.5 75.7 %reduce-scatter.3.cloned.1.call-start = ((), (), s32[]{:S(2)}) async-start(), calls=%async_computation.3 | async-start | bytes 7864320 | tf_op jit(solution)/shard_map/reduce_scatter | solution.py:51
  18.2 122.3 %reduce-scatter.5.cloned.1.call-start = ((), (), s32[]{:S(2)}) async-start(), calls=%async_computation.4 | async-start | bytes 7864320 | tf_op jit(solution)/shard_map/reduce_scatter | solution.py:52
  30.2 0.8 copy-start.2
  30.2 34.2 %copy-start.7 = (u32[32]{0:T(128)S(1)}, u32[32]{0:T(128)}, u32[]{:S(2)}) copy-start(u32[32]{0:T(128)} %constant.67) | copy-start | bytes 388
  30.2 35.4 %copy-start.6 = (s32[12]{0:T(128)S(1)}, s32[12]{0:T(128)}, u32[]{:S(2)}) copy-start(s32[12]{0:T(128)} %param.11) | copy-start | bytes 148
  77.3 4.0 %copy-start.3 = (s32[12]{0:T(128)S(1)}, s32[12]{0:T(128)}, u32[]{:S(2)}) copy-start(s32[12]{0:T(128)} %param.12) | copy-start | bytes 148
  77.3 4.1 %copy-start.4 = (s32[8]{0:T(128)S(1)}, s32[8]{0:T(128)}, u32[]{:S(2)}) copy-start(s32[8]{0:T(128)} %param.18) | copy-start | bytes 100
  84.3 1.8 %copy-start.5 = (f32[128]{0:T(128)S(1)}, f32[128]{0:T(128)}, u32[]{:S(2)}) copy-start(f32[128]{0:T(128)} %param.15) | copy-start | bytes 1540
  142.6 8.2 %copy-start = (bf16[8,512,256]{2,1,0:T(8,128)(2,1)S(1)}, bf16[8,512,256]{2,1,0:T(8,128)(2,1)}, u32[]{:S(2)}) copy-start(bf16[8,512,256]{2,1,0:T(8,128)(2,1)} %param.17) | copy-start | bytes 6291460
  145.2 20.0 %all-to-all-start = ((f32[16,2,2,8,129]{4,3,2,1,0:T(8,128)}), f32[16,2,2,8,129]{4,3,2,1,0:T(8,128)S(1)}, u32[]{:S(2)}, u32[]{:S(2)}) async-start(f32[16,2,2,8,129]{4,3,2,1,0:T(8,128)} %pad_maximum_fusion), calls=%async_computation.2 | async-start | bytes 1048576 | tf_op jit(solution)/shard_map/all_to_all | solution.py:72
  152.9 14.3 %copy-start.1 = (bf16[8,512,2,128]{3,2,1,0:T(2,128)(2,1)S(1)}, bf16[8,512,2,128]{3,2,1,0:T(2,128)(2,1)}, u32[]{:S(2)}) copy-start(bf16[8,512,2,128]{3,2,1,0:T(2,128)(2,1)} %reshape.249) | copy-start | bytes 6291460
Sparse Core Ops, SparseCore 0:
  18.4 61.0 reduce-scatter.2
  82.1 58.3 reduce-scatter.4

commit v2 on v1

v2 whole, which is shorter than its diff:
```python
import functools

import jax
import jax.numpy as jnp
from jax import lax
from jax.experimental import pallas as pl
from jax.experimental.pallas import tpu as pltpu
from jax.sharding import PartitionSpec as P

KVH = 8
NH = 64
HD = 128
EPSILON = 1e-05
FLOOR = -1e30
CORES = 2
CORE_TYPE = jnp.float32
MESH = pl.DeviceIdType.MESH


def attend(query, keys, values, live_count):
    scores = lax.dot_general(
        query, keys, (((1,), (1,)), ((), ())), preferred_element_type=jnp.float32
    ) * (HD ** -0.5)
    live = lax.broadcasted_iota(jnp.int32, scores.shape, 1) < live_count
    scores = jnp.where(live, scores, FLOOR)
    peak = jnp.max(scores, axis=1, keepdims=True)
    weights = jnp.where(live, jnp.exp(scores - peak), 0.0)
    total = jnp.sum(weights, axis=1, keepdims=True)
    out = jnp.dot(weights.astype(jnp.bfloat16), values, preferred_element_type=jnp.float32)
    some = total > 0
    safe = jnp.where(some, total, 1.0)
    return out / safe, jnp.where(some, peak + jnp.log(safe), FLOOR)


def kernel(
    groups, tensor, tiles, tile_len, requests, chunks,
    req_ref, rows_ref, len_ref, gain_ref, q_ref, feat_ref, kw_ref, vw_ref, ck_ref, cv_ref,
    out_ref,
    fbuf, wbuf, ckbuf, cvbuf, allq, csend, crecv, own, keep, ysend, yrecv,
    cache_out, cache_lse, tile_out, tile_lse, send_out, send_lse, got_out, got_lse, slot_lse, slot_req,
    fsem, wsem, csem, qsend, qrecv, cs_sem, cr_sem, ys_sem, yr_sem, os_sem, or_sem, ls_sem, lr_sem,
):
    ys = tensor // CORES
    heads = KVH // tensor
    width = heads * HD
    chunk = tiles * tile_len // chunks
    per_chunk = tiles // chunks
    peer_slots = -(-tiles // groups)
    qrows = q_ref.shape[2]
    me = lax.axis_index("grp")
    tp = lax.axis_index("tp")
    y, core = tp // CORES, tp % CORES
    partner = y * CORES + (1 - core)

    def y_peer(k):
        return lax.rem(y + k, ys) * CORES + core

    def grp_peer(k):
        return lax.rem(me + k, groups)

    def feat_copy(i):
        return pltpu.make_async_copy(
            feat_ref.at[pl.ds(pl.multiple_of(i * chunk, chunk), chunk)], fbuf.at[i], fsem.at[i]
        )

    def weight_copy(side, k, kv):
        col_core = (1 - core) if side == 0 else core
        col = pl.multiple_of((lax.rem(y + k, ys) * CORES + col_core) * width, width)
        return pltpu.make_async_copy(
            (kw_ref, vw_ref)[kv].at[:, pl.ds(col, width)], wbuf.at[side, k, kv], wsem.at[side, k, kv]
        )

    order = [k % ys for k in range(1, ys + 1)]
    feat_copy(0).start()
    for side in range(2):
        for k in order:
            for kv in range(2):
                weight_copy(side, k, kv).start()
        if side == 0:
            for i in range(1, chunks):
                feat_copy(i).start()
    key_copy = pltpu.make_async_copy(ck_ref, ckbuf, csem.at[0])
    value_copy = pltpu.make_async_copy(cv_ref, cvbuf, csem.at[1])
    key_copy.start()
    value_copy.start()

    barrier = pltpu.get_barrier_semaphore()
    pl.semaphore_signal(barrier, inc=1, device_id={"tp": partner}, device_id_type=MESH)
    for k in range(1, ys):
        pl.semaphore_signal(barrier, inc=1, device_id={"tp": y_peer(k)}, device_id_type=MESH)
    for k in range(1, groups):
        pl.semaphore_signal(barrier, inc=1, device_id={"grp": grp_peer(k)}, device_id_type=MESH)
    pl.semaphore_wait(barrier, 1 + (ys - 1) + (groups - 1))

    allq[pl.ds(pl.multiple_of(me * requests, requests), requests)] = q_ref[...]

    def query_copy(k):
        return pltpu.make_async_remote_copy(
            src_ref=q_ref,
            dst_ref=allq.at[pl.ds(pl.multiple_of(me * requests, requests), requests)],
            send_sem=qsend.at[k], recv_sem=qrecv.at[k],
            device_id={"grp": grp_peer(k)}, device_id_type=MESH,
        )

    for k in range(1, groups):
        query_copy(k).start()

    def core_copy(i):
        return pltpu.make_async_remote_copy(
            src_ref=csend.at[i], dst_ref=crecv.at[i],
            send_sem=cs_sem.at[i], recv_sem=cr_sem.at[i],
            device_id={"tp": partner}, device_id_type=MESH,
        )

    def y_copy(i, k):
        return pltpu.make_async_remote_copy(
            src_ref=ysend.at[i, k - 1], dst_ref=yrecv.at[i, k - 1],
            send_sem=ys_sem.at[i, k - 1], recv_sem=yr_sem.at[i, k - 1],
            device_id={"tp": y_peer(k)}, device_id_type=MESH,
        )

    def give(i, wait):
        for k in order:
            for kv in range(2):
                if wait:
                    weight_copy(0, k, kv).wait()
                csend[i, k, kv] = jnp.dot(
                    fbuf[i], wbuf[0, k, kv], preferred_element_type=jnp.float32
                ).astype(csend.dtype)
        core_copy(i).start()

    feat_copy(0).wait()
    give(0, True)
    for k in order:
        for kv in range(2):
            weight_copy(1, k, kv).wait()

    def step(i, carry):
        for k in order:
            for kv in range(2):
                own[k, kv] = jnp.dot(fbuf[i], wbuf[1, k, kv], preferred_element_type=jnp.float32)

        @pl.when(i + 1 < chunks)
        def _():
            feat_copy(i + 1).wait()
            give(i + 1, False)

        core_copy(i).wait_recv()
        for k in range(1, ys):
            ysend[i, k - 1] = (own[k] + crecv[i, k].astype(jnp.float32)).astype(jnp.bfloat16)
            y_copy(i, k).start()
        keep[i] = own[0] + crecv[i, 0].astype(jnp.float32)
        return carry

    lax.fori_loop(0, chunks, step, 0)

    key_copy.wait()
    value_copy.wait()

    def cached(r, carry):
        for h in range(heads):
            cols = pl.ds(h * HD, HD)
            o, lse = attend(q_ref[r, h], ckbuf[r, :, cols], cvbuf[r, :, cols], len_ref[r])
            cache_out[r, h] = o
            cache_lse[r, h] = jnp.broadcast_to(lse, (qrows, HD))
        return carry

    lax.fori_loop(0, requests, cached, 0)
    for k in range(1, groups):
        query_copy(k).wait()

    gain = gain_ref[...]

    def fresh(i, carry):
        for k in range(1, ys):
            y_copy(i, k).wait_recv()
        for u in range(per_chunk):
            t = i * per_chunk + u
            rows = pl.ds(u * tile_len, tile_len)
            for h in range(heads):
                cols = pl.ds(h * HD, HD)
                raw_k = keep[i, 0, rows, cols]
                raw_v = keep[i, 1, rows, cols]
                for k in range(1, ys):
                    raw_k = raw_k + yrecv[i, k - 1, 0, rows, cols].astype(jnp.float32)
                    raw_v = raw_v + yrecv[i, k - 1, 1, rows, cols].astype(jnp.float32)
                scale = lax.rsqrt(jnp.mean(raw_k * raw_k, axis=1, keepdims=True) + EPSILON)
                new_k = (raw_k * scale * gain).astype(jnp.bfloat16)
                o, lse = attend(allq[req_ref[t], h], new_k, raw_v.astype(jnp.bfloat16), rows_ref[t])
                tile_out[t, h] = o.astype(jnp.bfloat16)
                tile_lse[t, h] = jnp.broadcast_to(lse, (qrows, HD))
        return carry

    lax.fori_loop(0, chunks, fresh, 0)

    reqs = [req_ref[t] for t in range(tiles)]
    targets = [r // requests for r in reqs]
    ranks = []
    for t in range(tiles):
        rank = jnp.int32(0)
        for s in range(t):
            rank = rank + (targets[s] == targets[t]).astype(jnp.int32)
        ranks.append(rank)
    lane = lax.broadcasted_iota(jnp.int32, (heads, qrows, HD), 2)

    def out_copy(k):
        return pltpu.make_async_remote_copy(
            src_ref=send_out.at[k], dst_ref=got_out.at[k],
            send_sem=os_sem.at[k], recv_sem=or_sem.at[k],
            device_id={"grp": grp_peer(k)}, device_id_type=MESH,
        )

    def lse_copy(k):
        return pltpu.make_async_remote_copy(
            src_ref=send_lse.at[k], dst_ref=got_lse.at[k],
            send_sem=ls_sem.at[k], recv_sem=lr_sem.at[k],
            device_id={"grp": grp_peer(k)}, device_id_type=MESH,
        )

    for k in list(range(1, groups)) + [0]:
        group = grp_peer(k)
        packed = jnp.full((heads, qrows, HD), FLOOR, jnp.float32)
        o_to, l_to = (send_out, send_lse) if k else (got_out, got_lse)
        for j in range(peer_slots):
            source = jnp.int32(0)
            found = jnp.int32(0)
            for t in range(tiles):
                here = ((targets[t] == group) & (ranks[t] == j)).astype(jnp.int32)
                source = source + here * t
                found = found + here
            o_to[k, j] = tile_out[source]
            local = jnp.where(found > 0, req_ref[source] - group * requests, -1)
            lse = jnp.where(found > 0, tile_lse[source], FLOOR)
            packed = jnp.where(lane == j, lse, packed)
            packed = jnp.where(lane == HD // 2 + j, local.astype(jnp.float32), packed)
        l_to[k] = packed
        if k:
            lse_copy(k).start()
            out_copy(k).start()

    for i in range(chunks):
        core_copy(i).wait_send()
        for k in range(1, ys):
            y_copy(i, k).wait_send()
    for k in range(1, groups):
        lse_copy(k).wait()
        out_copy(k).wait()

    for k in range(groups):
        for j in range(peer_slots):
            s = k * peer_slots + j
            slot_lse[s] = jnp.broadcast_to(got_lse[k, :, :, j : j + 1], (heads, qrows, HD))
            slot_req[s] = jnp.broadcast_to(
                got_lse[k, :, :, HD // 2 + j : HD // 2 + j + 1], (heads, qrows, HD)
            )

    def merge(r, carry):
        want = r.astype(jnp.float32)
        base = cache_lse[r]
        peak = base
        for s in range(groups * peer_slots):
            peak = jnp.maximum(peak, jnp.where(slot_req[s] == want, slot_lse[s], FLOOR))
        weight = jnp.exp(base - peak)
        num = weight * cache_out[r]
        den = weight
        for k in range(groups):
            for j in range(peer_slots):
                s = k * peer_slots + j
                mine = slot_req[s] == want
                weight = jnp.where(mine, jnp.exp(jnp.where(mine, slot_lse[s], FLOOR) - peak), 0.0)
                num = num + weight * got_out[k, j].astype(jnp.float32)
                den = den + weight
        out_ref[r] = (num / den).astype(jnp.bfloat16)
        return carry

    lax.fori_loop(0, requests, merge, 0)


def on_device(
    features, tile_request, tile_rows, key_weight, value_weight, key_gain,
    cached_keys, cached_values, cache_len, queries,
):
    groups = lax.axis_size("grp")
    tensor = lax.axis_size("tp")
    tiles, tile_len, feat = features.shape
    ys = tensor // CORES
    heads = KVH // tensor
    width = heads * HD
    per = NH // KVH
    steps = queries.shape[0]
    requests = cache_len.shape[0]
    cache_slots = cached_keys.shape[1]
    peer_slots = -(-tiles // groups)
    qrows = steps * per
    chunks = 6 if tiles % 6 == 0 else tiles
    chunk = tiles * tile_len // chunks
    hops = max(ys - 1, 1)
    q = queries.reshape(steps, requests, heads, per, HD).transpose(1, 2, 0, 3, 4)
    q = q.reshape(requests, heads, qrows, HD)
    bf, f32 = jnp.bfloat16, jnp.float32
    vmem = pl.BlockSpec(memory_space=pltpu.VMEM)
    smem = pl.BlockSpec(memory_space=pltpu.SMEM)
    hbm = pl.BlockSpec(memory_space=pl.ANY)
    dma = pltpu.SemaphoreType.DMA
    slots = groups * peer_slots
    out = pl.pallas_call(
        functools.partial(kernel, groups, tensor, tiles, tile_len, requests, chunks),
        out_shape=jax.ShapeDtypeStruct((requests, heads, qrows, HD), bf),
        in_specs=[smem, smem, smem, vmem, vmem, hbm, hbm, hbm, hbm, hbm],
        out_specs=vmem,
        scratch_shapes=[
            pltpu.VMEM((chunks, chunk, feat), bf),
            pltpu.VMEM((2, ys, 2, feat, width), bf),
            pltpu.VMEM((requests, cache_slots, width), bf),
            pltpu.VMEM((requests, cache_slots, width), bf),
            pltpu.VMEM((groups * requests, heads, qrows, HD), bf),
            pltpu.VMEM((chunks, ys, 2, chunk, width), CORE_TYPE),
            pltpu.VMEM((chunks, ys, 2, chunk, width), CORE_TYPE),
            pltpu.VMEM((ys, 2, chunk, width), f32),
            pltpu.VMEM((chunks, 2, chunk, width), f32),
            pltpu.VMEM((chunks, hops, 2, chunk, width), bf),
            pltpu.VMEM((chunks, hops, 2, chunk, width), bf),
            pltpu.VMEM((requests, heads, qrows, HD), f32),
            pltpu.VMEM((requests, heads, qrows, HD), f32),
            pltpu.VMEM((tiles, heads, qrows, HD), bf),
            pltpu.VMEM((tiles, heads, qrows, HD), f32),
            pltpu.VMEM((groups, peer_slots, heads, qrows, HD), bf),
            pltpu.VMEM((groups, heads, qrows, HD), f32),
            pltpu.VMEM((groups, peer_slots, heads, qrows, HD), bf),
            pltpu.VMEM((groups, heads, qrows, HD), f32),
            pltpu.VMEM((slots, heads, qrows, HD), f32),
            pltpu.VMEM((slots, heads, qrows, HD), f32),
            dma((chunks,)), dma((2, ys, 2)), dma((2,)),
            dma((groups,)), dma((groups,)),
            dma((chunks,)), dma((chunks,)),
            dma((chunks, hops)), dma((chunks, hops)),
            dma((groups,)), dma((groups,)), dma((groups,)), dma((groups,)),
        ],
        compiler_params=pltpu.CompilerParams(
            collective_id=0, has_side_effects=True, vmem_limit_bytes=60 * 1024 * 1024
        ),
    )(
        tile_request, tile_rows, cache_len, key_gain.reshape(1, HD), q,
        features.reshape(tiles * tile_len, feat), key_weight, value_weight, cached_keys, cached_values,
    )
    out = out.reshape(requests, heads, steps, per, HD).transpose(2, 0, 1, 3, 4)
    return out.reshape(steps, requests, heads * per * HD)


def solution(mesh):
    in_specs = (
        P("grp", None, "tp"), P("grp"), P("grp"), P("tp", None), P("tp", None), P(),
        P("grp", None, "tp"), P("grp", None, "tp"), P("grp"), P(None, "grp", "tp"),
    )
    return jax.shard_map(
        on_device, mesh=mesh, in_specs=in_specs, out_specs=P(None, "grp", "tp"), check_vma=False
    )
```

time: 176 us -> 62.2 us (0.35)
  waiting for transfers between devices: 63.5 us -> 0 us
  Pallas kernels: 0 us -> 59 us
  blocking collectives: 43.9 us -> 0 us
  matrix products: 25.8 us -> 0 us
  between operations: 14.4 us -> 0.01 us
  other arithmetic: 9.6 us -> 0 us
  local copies, waits for them, and re-layouts: 12.5 us -> 2.97 us
  starting transfers between devices: 5.53 us -> 0 us
    pallas_call x0 -> x1, Pallas kernels: none -> 59 us  [on_device(): pl.pallas_call(functools.partial(kernel, groups, tensor, tiles, tile_len,...]
    reduce_scatter x2 -> x0, waiting for transfers between devices: 51.5 us -> none  [the longest x1 51.5 us: on_device(): lax.psum_scatter(part_values, 'tp', scatter_dimension=1, tiled=True)]
    all_gather x1 -> x0, blocking collectives: 33.1 us -> none  [on_device(): all_q = lax.all_gather(queries, 'grp', axis=0, tiled=False)]
    dot_general x6 -> x0, matrix products: 25.8 us -> none  [the longest x1 11.9 us: on_device(): jnp.dot(flat, value_weight, preferred_element_type=jnp.float32)]
    all_to_all x1 -> x0, waiting for transfers between devices: 12 us -> none  [on_device(): lax.all_to_all(payload, 'grp', split_axis=0, concat_axis=0, tiled=True)]
    unnamed x1 -> x0, blocking collectives: 10.8 us -> none
    reshape x6 -> x1, local copies, waits for them, and re-layouts: 7.66 us -> 1.48 us  [on_device(): queries.reshape(steps, requests, heads, per, HD).transpose(1, 2, 0, 3, 4)]
    all_to_all x1 -> x0, starting transfers between devices: 5.49 us -> none  [on_device(): lax.all_to_all(payload, 'grp', split_axis=0, concat_axis=0, tiled=True)]
  transfers between devices with their start and end apart: 3 -> 0, of which waited for: 2 -> 0; matrix products, arithmetic and copies ran while one was open for 16% -> 0% of each run, Pallas kernels for 0% -> 0%
where the time goes in v2:
time: 62.2 us; the launch traced here: 61.9 us
  Pallas kernels  59 us (95%)
  local copies, waits for them, and re-layouts  2.97 us (5%)
    pallas_call x1, Pallas kernels, on_device(): pl.pallas_call(functools.partial(kernel, groups, tensor, tiles, tile_len,...  59 us
    transpose x1, local copies, waits for them, and re-layouts, on_device(): out = out.reshape(requests, heads, steps, per, HD).transpose(2, 0, 1, 3, 4)  1.5 us
    reshape x1, local copies, waits for them, and re-layouts, on_device(): queries.reshape(steps, requests, heads, per, HD).transpose(1, 2, 0, 3, 4)  1.48 us

profile of v2, /device:TPU:0, one launch (start us, length us, event | category | flops | bytes accessed | tf_op | source)
XLA Modules:
  0.0 61.9 jit_solution(9283662123392101438)
XLA Ops:
  0.0 1.5 %copy.14 = bf16[2,8,2,8,128]{4,3,0,2,1:T(8,128)(2,1)} copy(bf16[2,8,2,8,128]{4,1,3,2,0:T(8,128)(2,1)} %bitcast.15) | data formatting | bytes 131072 | tf_op jit(solution)/shard_map/reshape | solution.py:298
  1.5 59.0 %shard_map.100 = bf16[8,2,16,128]{3,2,1,0:T(8,128)(2,1)} custom-call(s32[12]{0:T(128)} %req_ref.1, s32[12]{0:T(128)} %rows_ref.1, s32[8]{0:T(128)} %len_ref.1, f32[1,128]{1,0:T(1,128)} %bitcast.16, bf16[8,2,16,128]{3,2,1,0:T(8,128)(2,1)} %bitcast.14, bf16[1536,2048]{1,0:T(8,128)(2,1)} %bitcast.12, bf16[2048,1024]{1,0:T(8,128)(2,1)} %kw_ref.1, ...), custom_call_target="tpu_custom_call" | custom-call | tf_op jit(solution)/shard_map/pallas_call | solution.py:306
  60.4 1.5 %copy.12 = bf16[2,8,2,8,128]{4,1,3,2,0:T(8,128)(2,1)} copy(bf16[2,8,2,8,128]{4,3,0,2,1:T(8,128)(2,1)} %bitcast.13) | data formatting | bytes 131072 | tf_op jit(solution)/shard_map/transpose | solution.py:346

commit v3 on v2

--- a/solution.py
+++ b/solution.py
@@ -34,9 +34,9 @@
 
 def kernel(
     groups, tensor, tiles, tile_len, requests, chunks,
-    req_ref, rows_ref, len_ref, gain_ref, q_ref, feat_ref, kw_ref, vw_ref, ck_ref, cv_ref,
+    req_ref, rows_ref, len_ref, gain_ref, qin_ref, feat_ref, kw_ref, vw_ref, ck_ref, cv_ref,
     out_ref,
-    fbuf, wbuf, ckbuf, cvbuf, allq, csend, crecv, own, keep, ysend, yrecv,
+    q_ref, fbuf, wbuf, ckbuf, cvbuf, allq, csend, crecv, own, keep, ysend, yrecv,
     cache_out, cache_lse, tile_out, tile_lse, send_out, send_lse, got_out, got_lse, slot_lse, slot_req,
     fsem, wsem, csem, qsend, qrecv, cs_sem, cr_sem, ys_sem, yr_sem, os_sem, or_sem, ls_sem, lr_sem,
 ):
@@ -47,6 +47,8 @@
     per_chunk = tiles // chunks
     peer_slots = -(-tiles // groups)
     qrows = q_ref.shape[2]
+    steps = qin_ref.shape[0]
+    per = qrows // steps
     me = lax.axis_index("grp")
     tp = lax.axis_index("tp")
     y, core = tp // CORES, tp % CORES
@@ -57,6 +59,13 @@
 
     def grp_peer(k):
         return lax.rem(me + k, groups)
+
+    barrier = pltpu.get_barrier_semaphore()
+    pl.semaphore_signal(barrier, inc=1, device_id={"tp": partner}, device_id_type=MESH)
+    for k in range(1, ys):
+        pl.semaphore_signal(barrier, inc=1, device_id={"tp": y_peer(k)}, device_id_type=MESH)
+    for k in range(1, groups):
+        pl.semaphore_signal(barrier, inc=1, device_id={"grp": grp_peer(k)}, device_id_type=MESH)
 
     def feat_copy(i):
         return pltpu.make_async_copy(
@@ -84,14 +93,20 @@
     key_copy.start()
     value_copy.start()
 
-    barrier = pltpu.get_barrier_semaphore()
-    pl.semaphore_signal(barrier, inc=1, device_id={"tp": partner}, device_id_type=MESH)
-    for k in range(1, ys):
-        pl.semaphore_signal(barrier, inc=1, device_id={"tp": y_peer(k)}, device_id_type=MESH)
-    for k in range(1, groups):
-        pl.semaphore_signal(barrier, inc=1, device_id={"grp": grp_peer(k)}, device_id_type=MESH)
-    pl.semaphore_wait(barrier, 1 + (ys - 1) + (groups - 1))
-
+    total_rows = requests * qrows
+    to = lax.broadcasted_iota(jnp.int32, (total_rows, total_rows), 0)
+    frm = lax.broadcasted_iota(jnp.int32, (total_rows, total_rows), 1)
+    swap = (lax.div(to, qrows) == lax.rem(frm, requests)) & (lax.rem(to, qrows) == lax.div(frm, requests))
+    swap = jnp.where(swap, 1.0, 0.0).astype(jnp.bfloat16)
+    for h in range(heads):
+        rows = [
+            qin_ref[s, :, pl.ds((h * per + g) * HD, HD)].astype(jnp.float32)
+            for s in range(steps) for g in range(per)
+        ]
+        rows = jnp.concatenate(rows, axis=0).astype(jnp.bfloat16)
+        rows = jnp.dot(swap, rows, preferred_element_type=jnp.float32).astype(jnp.bfloat16)
+        for q in range(requests):
+            q_ref[q, h] = rows[q * qrows : (q + 1) * qrows]
     allq[pl.ds(pl.multiple_of(me * requests, requests), requests)] = q_ref[...]
 
     def query_copy(k):
@@ -102,8 +117,6 @@
             device_id={"grp": grp_peer(k)}, device_id_type=MESH,
         )
 
-    for k in range(1, groups):
-        query_copy(k).start()
 
     def core_copy(i):
         return pltpu.make_async_remote_copy(
@@ -127,10 +140,14 @@
                 csend[i, k, kv] = jnp.dot(
                     fbuf[i], wbuf[0, k, kv], preferred_element_type=jnp.float32
                 ).astype(csend.dtype)
+        if wait:
+            pl.semaphore_wait(barrier, 1 + (ys - 1) + (groups - 1))
         core_copy(i).start()
 
     feat_copy(0).wait()
     give(0, True)
+    for k in range(1, groups):
+        query_copy(k).start()
     for k in order:
         for kv in range(2):
             weight_copy(1, k, kv).wait()
@@ -201,6 +218,7 @@
         for s in range(t):
             rank = rank + (targets[s] == targets[t]).astype(jnp.int32)
         ranks.append(rank)
+    lanes = send_lse.shape[1]
     lane = lax.broadcasted_iota(jnp.int32, (heads, qrows, HD), 2)
 
     def out_copy(k):
@@ -232,8 +250,8 @@
             local = jnp.where(found > 0, req_ref[source] - group * requests, -1)
             lse = jnp.where(found > 0, tile_lse[source], FLOOR)
             packed = jnp.where(lane == j, lse, packed)
-            packed = jnp.where(lane == HD // 2 + j, local.astype(jnp.float32), packed)
-        l_to[k] = packed
+            packed = jnp.where(lane == peer_slots + j, local.astype(jnp.float32), packed)
+        l_to[k] = jnp.transpose(packed.reshape(heads * qrows, HD))[:lanes, :]
         if k:
             lse_copy(k).start()
             out_copy(k).start()
@@ -247,12 +265,13 @@
         out_copy(k).wait()
 
     for k in range(groups):
+        flat = jnp.transpose(got_lse[k])
         for j in range(peer_slots):
             s = k * peer_slots + j
-            slot_lse[s] = jnp.broadcast_to(got_lse[k, :, :, j : j + 1], (heads, qrows, HD))
-            slot_req[s] = jnp.broadcast_to(
-                got_lse[k, :, :, HD // 2 + j : HD // 2 + j + 1], (heads, qrows, HD)
-            )
+            lse = jnp.broadcast_to(flat[:, j : j + 1], (heads * qrows, HD))
+            local = jnp.broadcast_to(flat[:, peer_slots + j : peer_slots + j + 1], (heads * qrows, HD))
+            slot_lse[s] = lse.reshape(heads, qrows, HD)
+            slot_req[s] = local.reshape(heads, qrows, HD)
 
     def merge(r, carry):
         want = r.astype(jnp.float32)
@@ -292,23 +311,23 @@
     cache_slots = cached_keys.shape[1]
     peer_slots = -(-tiles // groups)
     qrows = steps * per
-    chunks = 6 if tiles % 6 == 0 else tiles
+    chunks = tiles
     chunk = tiles * tile_len // chunks
     hops = max(ys - 1, 1)
-    q = queries.reshape(steps, requests, heads, per, HD).transpose(1, 2, 0, 3, 4)
-    q = q.reshape(requests, heads, qrows, HD)
     bf, f32 = jnp.bfloat16, jnp.float32
     vmem = pl.BlockSpec(memory_space=pltpu.VMEM)
     smem = pl.BlockSpec(memory_space=pltpu.SMEM)
     hbm = pl.BlockSpec(memory_space=pl.ANY)
     dma = pltpu.SemaphoreType.DMA
     slots = groups * peer_slots
+    lanes = -(-2 * peer_slots // 8) * 8
     out = pl.pallas_call(
         functools.partial(kernel, groups, tensor, tiles, tile_len, requests, chunks),
         out_shape=jax.ShapeDtypeStruct((requests, heads, qrows, HD), bf),
         in_specs=[smem, smem, smem, vmem, vmem, hbm, hbm, hbm, hbm, hbm],
         out_specs=vmem,
         scratch_shapes=[
+            pltpu.VMEM((requests, heads, qrows, HD), bf),
             pltpu.VMEM((chunks, chunk, feat), bf),
             pltpu.VMEM((2, ys, 2, feat, width), bf),
             pltpu.VMEM((requests, cache_slots, width), bf),
@@ -325,9 +344,9 @@
             pltpu.VMEM((tiles, heads, qrows, HD), bf),
             pltpu.VMEM((tiles, heads, qrows, HD), f32),
             pltpu.VMEM((groups, peer_slots, heads, qrows, HD), bf),
-            pltpu.VMEM((groups, heads, qrows, HD), f32),
+            pltpu.VMEM((groups, lanes, heads * qrows), f32),
             pltpu.VMEM((groups, peer_slots, heads, qrows, HD), bf),
-            pltpu.VMEM((groups, heads, qrows, HD), f32),
+            pltpu.VMEM((groups, lanes, heads * qrows), f32),
             pltpu.VMEM((slots, heads, qrows, HD), f32),
             pltpu.VMEM((slots, heads, qrows, HD), f32),
             dma((chunks,)), dma((2, ys, 2)), dma((2,)),
@@ -340,7 +359,7 @@
             collective_id=0, has_side_effects=True, vmem_limit_bytes=60 * 1024 * 1024
         ),
     )(
-        tile_request, tile_rows, cache_len, key_gain.reshape(1, HD), q,
+        tile_request, tile_rows, cache_len, key_gain.reshape(1, HD), queries,
         features.reshape(tiles * tile_len, feat), key_weight, value_weight, cached_keys, cached_values,
     )
     out = out.reshape(requests, heads, steps, per, HD).transpose(2, 0, 1, 3, 4)

time: 62.2 us -> 57.6 us (0.926)
  Pallas kernels: 59 us -> 55.9 us
  local copies, waits for them, and re-layouts: 2.97 us -> 1.5 us
    pallas_call x1, Pallas kernels: 59 us -> 55.9 us  [on_device(): pl.pallas_call(functools.partial(kernel, groups, tensor, tiles, tile_len,...]
    reshape x1 -> x0, local copies, waits for them, and re-layouts: 1.48 us -> none  [on_device(): queries.reshape(steps, requests, heads, per, HD).transpose(1, 2, 0, 3, 4)]
where the time goes in v3:
time: 57.6 us; the launch traced here: 57.4 us
  Pallas kernels  55.9 us (97%)
  local copies, waits for them, and re-layouts  1.5 us (3%)
    pallas_call x1, Pallas kernels, on_device(): pl.pallas_call(functools.partial(kernel, groups, tensor, tiles, tile_len,...  55.9 us
    transpose x1, local copies, waits for them, and re-layouts, on_device(): out = out.reshape(requests, heads, steps, per, HD).transpose(2, 0, 1, 3, 4)  1.5 us

profile of v3, /device:TPU:0, one launch (start us, length us, event | category | flops | bytes accessed | tf_op | source)
XLA Modules:
  0.0 57.4 jit_solution(8374559152574427579)
XLA Ops:
  0.0 55.9 %shard_map.100 = bf16[8,2,16,128]{3,2,1,0:T(8,128)(2,1)} custom-call(s32[12]{0:T(128)} %req_ref.1, s32[12]{0:T(128)} %rows_ref.1, s32[8]{0:T(128)} %len_ref.1, f32[1,128]{1,0:T(1,128)} %bitcast.8, bf16[2,8,2048]{2,1,0:T(8,128)(2,1)} %qin_ref.1, bf16[1536,2048]{1,0:T(8,128)(2,1)} %bitcast.6, bf16[2048,1024]{1,0:T(8,128)(2,1)} %kw_ref.1, ...), custom_call_target="tpu_custom_call" | custom-call | tf_op jit(solution)/shard_map/pallas_call | solution.py:324
  55.9 1.5 %copy.11 = bf16[2,8,2,8,128]{4,1,3,2,0:T(8,128)(2,1)} copy(bf16[2,8,2,8,128]{4,3,0,2,1:T(8,128)(2,1)} %bitcast.7) | data formatting | bytes 131072 | tf_op jit(solution)/shard_map/transpose | solution.py:365
